TPU v7x, 32 devices: a whole 2x2x4 slice. The times are simulated.
32 devices in a mesh: seq: 8 (over y, x, core), tp: 4 (over z).
Axes of the slice: x: 2, y: 2, z: 4, core: 2. Of those that a mesh axis runs over, the one named last changes fastest.
Arguments:
- query_rows: bfloat16 [2048, 6144], P('seq', 'tp'), may hold values from -6 to 6
- key_rows: bfloat16 [2048, 6144], P('seq', 'tp'), may hold values from -6 to 6
- value_rows: bfloat16 [2048, 6144], P('seq', 'tp'), may hold values from -6 to 6
- log_decay: float32 [48, 2048], P('tp', 'seq'), as said below
- doc_starts: int32 [8, 3], P('seq'), may hold values from 0 to 256, as said below
- residual_in: bfloat16 [2048, 4096], P(('seq', 'tp')), may hold values from -6 to 6
- out_weight: bfloat16 [6144, 4096], P('tp'), may hold values from -0.078125 to 0.078125
- norm_gain: float32 [4096], replicated, may hold values from 0.5 to 1.5
Outputs:
- hidden_state: bfloat16 [2048, 4096], P(('seq', 'tp'))
- normed_state: bfloat16 [2048, 4096], P(('seq', 'tp'))
Inputs may be any that keep to these rules, and one draw needn't show every extreme that they name: `doc_starts`: each entry is a document's start offset within its shard; 256 marks an unused slot; the last entry of every row is 256; the first entry of shard 0 is 0; entries may repeat and need not be sorted. `log_decay`: every entry is negative.
All inputs are finite; a program needn't handle non-finite values.
Results may differ from a plain program's by a relative error of at most 0.022.
Values may be sent and summed in bfloat16 or wider, within the bound.
A program may use at most 64 MiB of HBM per device.

v0:
```python
import functools

import jax
import jax.numpy as jnp
from jax import lax
from jax.experimental import pallas as pl
from jax.experimental.pallas import tpu as pltpu
from jax.sharding import PartitionSpec as P

MESH = pl.DeviceIdType.MESH
F32 = jnp.float32
BF16 = jnp.bfloat16
SKEW = 2


def _nt(a, b):
    return lax.dot_general(a, b, (((1,), (1,)), ((), ())), preferred_element_type=F32)


def _tn(a, b):
    return lax.dot_general(a, b, (((0,), (0,)), ((), ())), preferred_element_type=F32)


def kernel(
    cfg,
    q_hbm, k_hbm, v_hbm, decay_hbm, starts_hbm, res_hbm, gain_hbm, w_hbm,
    hid_ref, norm_ref,
    q_ref, k_ref, v_ref, decay_ref, starts_ref, res_ref, gain_ref, wbuf, decay_pad, cum_rows, bias, cum_cols, carry_cols, intra, att,
    state_out, sibling_in, pair_out, pair_in, prefix_out, prefix_in, carried,
    part, from_left, from_right, x_ref,
    in_sem, w_sem, s0_send, s0_recv, s1_send, s1_recv, s2_send, s2_recv, s3_send, s3_recv, rs_send, left_recv, right_recv,
):
    ns, nt, heads, hd, span, m, chunks, width, rows = cfg
    per = hd // m
    sets = state_out.shape[0]
    set_heads = heads // sets
    body_rows = set_heads * per
    group = 3 if set_heads % 3 == 0 else 1
    me = lax.axis_index("seq")
    pairs, half = ns // 2, m // 2
    pair, core = me // 2, me % 2
    sibling = me + 1 - 2 * core
    t = lax.axis_index("tp")

    pairs_of = [(decay_hbm, decay_ref), (starts_hbm, starts_ref)]
    for g in range(sets):
        lanes = pl.ds(g * set_heads * hd, set_heads * hd)
        pairs_of += [(k_hbm.at[:, lanes], k_ref.at[:, lanes]), (v_hbm.at[:, lanes], v_ref.at[:, lanes])]
    pairs_of += [(q_hbm, q_ref), (res_hbm, res_ref), (gain_hbm, gain_ref)]
    loads = [
        pltpu.make_async_copy(src, dst, in_sem.at[i]) for i, (src, dst) in enumerate(pairs_of)
    ]
    load_decay, load_starts, *load_sets, load_q, load_res, load_gain = loads
    for load in loads:
        load.start()

    def w_copy(c):
        return pltpu.make_async_copy(
            w_hbm.at[:, pl.ds(pl.multiple_of(c * width, width), width)], wbuf.at[c], w_sem.at[c]
        )

    barrier = pltpu.get_barrier_semaphore()
    pl.semaphore_signal(barrier, inc=1, device_id={"seq": sibling}, device_id_type=MESH)
    for d in range(1, pairs):
        pl.semaphore_signal(
            barrier, inc=1, device_id={"seq": lax.rem(me + 2 * d, ns)}, device_id_type=MESH
        )

    @pl.when(t > 0)
    def _():
        pl.semaphore_signal(barrier, inc=1, device_id={"tp": t - 1}, device_id_type=MESH)

    @pl.when(t < nt - 1)
    def _():
        pl.semaphore_signal(barrier, inc=1, device_id={"tp": t + 1}, device_id_type=MESH)

    row_i = lax.broadcasted_iota(jnp.int32, (span, span), 0)
    col_i = lax.broadcasted_iota(jnp.int32, (span, span), 1)
    lower = row_i >= col_i
    decay_pad[...] = jnp.zeros_like(decay_pad)
    load_decay.wait()
    decay_pad[0:heads, :] = decay_ref[...]
    cum = lax.dot_general(
        decay_pad[...], lower.astype(F32), (((1,), (1,)), ((), ())),
        preferred_element_type=F32, precision=lax.Precision.HIGHEST,
    )
    cum_rows[...] = cum
    cum_t = cum.T
    load_starts.wait()
    pos_c = lax.broadcasted_iota(jnp.int32, (span, 128), 0)
    seg_c = jnp.zeros((span, 128), jnp.int32)
    seg_r = jnp.zeros((1, span), jnp.int32)
    pos_r = lax.broadcasted_iota(jnp.int32, (1, span), 1)
    last_seg = jnp.zeros((1, 128), jnp.int32)
    for e in range(starts_ref.shape[1]):
        start = starts_ref[0, e]
        seg_c = seg_c + jnp.where(pos_c >= start, 1, 0)
        seg_r = seg_r + jnp.where(pos_r >= start, 1, 0)
        last_seg = last_seg + jnp.where(
            jnp.full((1, 128), span - 1, jnp.int32) >= start, 1, 0
        )
    tail_t = jnp.where(seg_c == last_seg, jnp.exp(cum_t[span - 1 : span, :] - cum_t), 0.0)
    carry_t = jnp.where(seg_c == 0, jnp.exp(cum_t), 0.0)

    through = jnp.where(last_seg == 0, jnp.exp(cum[:, span - 1 : span]), 0.0)[0:16, :]
    hi = through.astype(BF16)
    lo = (through - hi.astype(F32)).astype(BF16)

    def local_states(g):
        for i in range(set_heads):
            h = g * set_heads + i
            lanes = slice(h * hd, (h + 1) * hd)
            dk = (k_ref[:, lanes].astype(F32) * tail_t[:, h : h + 1]).astype(BF16)
            local = _tn(dk, v_ref[:, lanes]).astype(BF16)
            for j in range(m):
                state_out[g, j % 2, j // 2, i * per : (i + 1) * per, :] = local[
                    j * per : (j + 1) * per, :
                ]
        for j in range(m):
            state_out[g, j % 2, j // 2, body_rows : body_rows + 16, :] = hi
            state_out[g, j % 2, j // 2, body_rows + 16 : body_rows + 32, :] = lo

    def s0_copy(g, whole):
        src, dst = state_out.at[g], sibling_in.at[g]
        return pltpu.make_async_remote_copy(
            src_ref=src if whole else src.at[0], dst_ref=dst if whole else dst.at[0],
            send_sem=s0_send.at[g], recv_sem=s0_recv.at[g],
            device_id={"seq": sibling}, device_id_type=MESH,
        )

    def s1_copy(g, i, p):
        return pltpu.make_async_remote_copy(
            src_ref=pair_out.at[g, i], dst_ref=pair_in.at[g, p], send_sem=s1_send.at[g, i],
            recv_sem=s1_recv.at[g, p], device_id={"seq": 2 * i + core}, device_id_type=MESH,
        )

    def s2_copy(g, p, i):
        return pltpu.make_async_remote_copy(
            src_ref=prefix_out.at[g, p], dst_ref=prefix_in.at[g, core, i],
            send_sem=s2_send.at[g, p], recv_sem=s2_recv.at[g, i],
            device_id={"seq": 2 * p + core}, device_id_type=MESH,
        )

    def s3_copy(g, c):
        return pltpu.make_async_remote_copy(
            src_ref=prefix_in.at[g, c], dst_ref=prefix_in.at[g, c], send_sem=s3_send.at[g],
            recv_sem=s3_recv.at[g], device_id={"seq": sibling}, device_id_type=MESH,
        )

    def send_states(g):
        @pl.when(core == 0)
        def _():
            s0_copy(g, True).start()

        @pl.when(core == 1)
        def _():
            s0_copy(g, False).start()

    def decays(block):
        tail = block[body_rows : body_rows + 32, :].astype(F32)
        return tail[0:16] + tail[16:32]

    def totals(g):
        def work(first, second, parity):
            thr0, thr1 = decays(first[g, parity, 0]), decays(second[g, parity, 0])
            both = thr0 * thr1
            both_hi = both.astype(BF16)
            both_lo = (both - both_hi.astype(F32)).astype(BF16)
            for d in range(half):
                for i in range(set_heads):
                    h = g * set_heads + i
                    rows_h = slice(i * per, (i + 1) * per)
                    pair_out[g, d, rows_h, :] = (
                        thr1[h : h + 1, :] * first[g, parity, d, rows_h, :].astype(F32)
                        + second[g, parity, d, rows_h, :].astype(F32)
                    ).astype(BF16)
                pair_out[g, d, body_rows : body_rows + 16, :] = both_hi
                pair_out[g, d, body_rows + 16 : body_rows + 32, :] = both_lo

        @pl.when(core == 0)
        def _():
            s0_copy(g, False).wait_recv()
            work(state_out, sibling_in, 0)

        @pl.when(core == 1)
        def _():
            s0_copy(g, True).wait_recv()
            work(sibling_in, state_out, 1)

        for d in range(half):
            i = lax.rem(pair + d, half)

            @pl.when((i != pair) & (pair < pairs - 1))
            def _():
                s1_copy(g, i, pair).start()

        @pl.when((pair < half) & (pair < pairs - 1))
        def _():
            pair_in[g, pair] = pair_out[g, pair]

    for load in load_sets[0:2]:
        load.wait()
    local_states(0)
    pl.semaphore_wait(
        barrier, pairs + jnp.where(t > 0, 1, 0) + jnp.where(t < nt - 1, 1, 0)
    )
    send_states(0)
    for load in load_sets[2:]:
        load.wait()
    for c in range(chunks):
        w_copy(c).start()
    for g in range(1, sets):
        local_states(g)
        send_states(g)

    for g in range(sets):
        totals(g)

    seg_full = jnp.concatenate([seg_c] * (span // 128), axis=1)
    bias[...] = jnp.where(lower & (seg_full == seg_r), 0.0, -jnp.inf)
    for h in range(heads):
        cum_cols[h] = jnp.broadcast_to(cum_t[:, h : h + 1], (span, 128))
        carry_cols[h] = jnp.broadcast_to(carry_t[:, h : h + 1], (span, 128))
    load_q.wait()

    def within(i, _):
        for o in range(group):
            h = i * group + o
            lanes = pl.ds(pl.multiple_of(h * hd, hd), hd)
            scores = _nt(q_ref[:, lanes], k_ref[:, lanes])
            cols = jnp.concatenate([cum_cols[h]] * (span // 128), axis=1)
            decay = jnp.exp(cols - cum_rows[pl.ds(h, 1), :] + bias[...])
            weights = (scores * decay).astype(BF16)
            intra[h] = jnp.dot(weights, v_ref[:, lanes], preferred_element_type=F32)
        return 0

    def scan(g):
        @pl.when(pair < half)
        def _():
            state = [jnp.zeros((per, hd), F32) for _ in range(set_heads)]
            for p in range(pairs - 1):

                @pl.when(pair != p)
                def _():
                    s1_copy(g, 0, p).wait_recv()

                thr = decays(pair_in[g, p])
                for i in range(set_heads):
                    h = g * set_heads + i
                    rows_h = slice(i * per, (i + 1) * per)
                    state[i] = thr[h : h + 1, :] * state[i] + pair_in[g, p, rows_h, :].astype(F32)
                    prefix_out[g, p + 1, rows_h, :] = state[i].astype(BF16)

                @pl.when(pair != p + 1)
                def _():
                    s2_copy(g, p + 1, pair).start()

            @pl.when(pair > 0)
            def _():
                prefix_in[g, core, pair] = prefix_out[g, pair]

        @pl.when(pair == 0)
        def _():
            prefix_in[g] = jnp.zeros_like(prefix_in[g])

    def share(g):
        @pl.when(pair > 0)
        def _():
            for i in range(half):

                @pl.when(pair != i)
                def _():
                    s2_copy(g, 0, i).wait_recv()

            s3_copy(g, core).start()

    def across(g):
        @pl.when(pair > 0)
        def _():
            s3_copy(g, 1 - core).wait_recv()

        @pl.when(core == 0)
        def _():
            for j in range(m):
                carried[g, j] = prefix_in[g, j % 2, j // 2]

        @pl.when(core == 1)
        def _():
            thr = decays(sibling_in[g, 0, 0])
            for j in range(m):
                for i in range(set_heads):
                    h = g * set_heads + i
                    rows_h = slice(i * per, (i + 1) * per)
                    carried[g, j, rows_h, :] = (
                        thr[h : h + 1, :] * prefix_in[g, j % 2, j // 2, rows_h, :].astype(F32)
                        + sibling_in[g, j % 2, j // 2, rows_h, :].astype(F32)
                    ).astype(BF16)

        def some(n, _):
            for o in range(group):
                i = n * group + o
                h = g * set_heads + i
                lanes = pl.ds(pl.multiple_of(h * hd, hd), hd)
                rows_h = pl.ds(pl.multiple_of(i * per, per), per)
                state = jnp.concatenate([carried[g, j, rows_h, :] for j in range(m)], axis=0)
                inter = jnp.dot(q_ref[:, lanes], state, preferred_element_type=F32)
                mixed = intra[h] + inter * carry_cols[h]
                mean = jnp.mean(mixed * mixed, axis=1, keepdims=True)
                att[:, lanes] = (mixed * lax.rsqrt(mean + 1e-06)).astype(BF16)
            return 0

        lax.fori_loop(0, set_heads // group, some, 0)

    per_set = set_heads // group
    lax.fori_loop(0, per_set, within, 0)
    for g in range(sets):
        scan(g)
    lax.fori_loop(per_set, sets * per_set, within, 0)
    for g in range(sets):
        share(g)
    for g in range(sets):
        across(g)

    def right_copy(b, c):
        return pltpu.make_async_remote_copy(
            src_ref=part.at[b, c], dst_ref=from_left.at[b, c], send_sem=rs_send.at[b, c],
            recv_sem=left_recv.at[b, c], device_id={"tp": jnp.minimum(t + 1, nt - 1)},
            device_id_type=MESH,
        )

    def left_copy(b, c):
        return pltpu.make_async_remote_copy(
            src_ref=part.at[b, c], dst_ref=from_right.at[b, c], send_sem=rs_send.at[b, c],
            recv_sem=right_recv.at[b, c], device_id={"tp": jnp.maximum(t - 1, 0)},
            device_id_type=MESH,
        )

    units = (nt - 1) * chunks

    def add_into(b, c, other):
        part[b, c] = (part[b, c].astype(F32) + other[b, c].astype(F32)).astype(BF16)

    def step(k, _):
        @pl.when(k < chunks)
        def _():
            w_copy(k).wait()
            out = jnp.dot(att[...], wbuf[k], preferred_element_type=F32).astype(BF16)
            for b in range(nt):
                part[b, k] = out[b * rows : (b + 1) * rows, :]

        ur = k - t * SKEW
        br = nt - 1 - ur // chunks
        cr = ur % chunks

        @pl.when((ur >= 0) & (ur < units) & (br > t))
        def _():
            @pl.when(t > 0)
            def _():
                right_copy(br, cr).wait_recv()
                add_into(br, cr, from_left)

            right_copy(br, cr).start()

        ul = k - (nt - 1 - t) * SKEW
        bl = ul // chunks
        cl = ul % chunks

        @pl.when((ul >= 0) & (ul < units) & (bl < t))
        def _():
            @pl.when(t < nt - 1)
            def _():
                left_copy(bl, cl).wait_recv()
                add_into(bl, cl, from_right)

            left_copy(bl, cl).start()

        return 0

    lax.fori_loop(0, units + (nt - 1) * SKEW, step, 0)

    load_res.wait()
    load_gain.wait()

    total = jnp.zeros((rows, 1), F32)
    for c in range(chunks):
        lanes = slice(c * width, (c + 1) * width)
        x_ref[c] = res_ref[:, lanes].astype(F32) + part[t, c].astype(F32)

        @pl.when(t > 0)
        def _():
            right_copy(t, c).wait_recv()
            x_ref[c] += from_left[t, c].astype(F32)

        @pl.when(t < nt - 1)
        def _():
            left_copy(t, c).wait_recv()
            x_ref[c] += from_right[t, c].astype(F32)

        x = x_ref[c]
        hid_ref[:, lanes] = x.astype(BF16)
        total = total + jnp.sum(x * x, axis=1, keepdims=True)
    scale = lax.rsqrt(total / (chunks * width) + 1e-05)
    for c in range(chunks):
        lanes = slice(c * width, (c + 1) * width)
        norm_ref[:, lanes] = (x_ref[c] * scale * gain_ref[:, lanes]).astype(BF16)

    for g in range(sets):

        @pl.when(core == 0)
        def _():
            s0_copy(g, True).wait_send()

        @pl.when(core == 1)
        def _():
            s0_copy(g, False).wait_send()

        for i in range(half):

            @pl.when((pair != i) & (pair < pairs - 1))
            def _():
                s1_copy(g, i, 0).wait_send()

        for p in range(1, pairs):

            @pl.when((pair != p) & (pair < half))
            def _():
                s2_copy(g, p, 0).wait_send()

        @pl.when(pair > 0)
        def _():
            s3_copy(g, core).wait_send()

    def drain(u, _):
        b = u // chunks
        c = u % chunks

        @pl.when(b != t)
        def _():
            right_copy(b, c).wait_send()

        return 0

    lax.fori_loop(0, nt * chunks, drain, 0)


def write_kernel(hid_ref, norm_ref, hid_hbm, norm_hbm, sem):
    copies = [
        pltpu.make_async_copy(hid_ref, hid_hbm, sem.at[0]),
        pltpu.make_async_copy(norm_ref, norm_hbm, sem.at[1]),
    ]
    for copy in copies:
        copy.start()
    for copy in copies:
        copy.wait()


def shards(ns, nt, query, key, value, log_decay, doc_starts, residual, weight, gain):
    span = query.shape[0]
    heads = log_decay.shape[0]
    hd = query.shape[1] // heads
    rows, depth = residual.shape
    m = min(ns, hd // 16)
    pairs, half = ns // 2, m // 2
    per = hd // m
    sets = 2 if heads % 2 == 0 else 1
    body = heads // sets * per
    chunks = 8
    width = depth // chunks
    cfg = (ns, nt, heads, hd, span, m, chunks, width, rows)
    vmem = pl.BlockSpec(memory_space=pltpu.VMEM)
    hbm = pl.BlockSpec(memory_space=pl.ANY)
    dma = pltpu.SemaphoreType.DMA
    outs = pl.pallas_call(
        functools.partial(kernel, cfg),
        out_shape=[pltpu.VMEM((rows, depth), BF16)] * 2,
        in_specs=[hbm] * 8,
        out_specs=[vmem, vmem],
        scratch_shapes=[
            pltpu.VMEM(query.shape, BF16),
            pltpu.VMEM(query.shape, BF16),
            pltpu.VMEM(query.shape, BF16),
            pltpu.VMEM(log_decay.shape, F32),
            pltpu.SMEM(doc_starts.shape, jnp.int32),
            pltpu.VMEM(residual.shape, BF16),
            pltpu.VMEM((1, depth), F32),
            pltpu.VMEM((chunks, weight.shape[0], width), BF16),
            pltpu.VMEM((128, span), F32),
            pltpu.VMEM((128, span), F32),
            pltpu.VMEM((span, span), F32),
            pltpu.VMEM((heads, span, 128), F32),
            pltpu.VMEM((heads, span, 128), F32),
            pltpu.VMEM((heads, span, hd), F32),
            pltpu.VMEM((span, heads * hd), BF16),
            pltpu.VMEM((sets, 2, half, body + 32, hd), BF16),
            pltpu.VMEM((sets, 2, half, body + 32, hd), BF16),
            pltpu.VMEM((sets, half, body + 32, hd), BF16),
            pltpu.VMEM((sets, pairs, body + 32, hd), BF16),
            pltpu.VMEM((sets, pairs, body, hd), BF16),
            pltpu.VMEM((sets, 2, half, body, hd), BF16),
            pltpu.VMEM((sets, m, body, hd), BF16),
            pltpu.VMEM((nt, chunks, rows, width), BF16),
            pltpu.VMEM((nt, chunks, rows, width), BF16),
            pltpu.VMEM((nt, chunks, rows, width), BF16),
            pltpu.VMEM((chunks, rows, width), F32),
            dma((5 + 2 * sets,)),
            dma((chunks,)),
            dma((sets,)),
            dma((sets,)),
            dma((sets, half)),
            dma((sets, pairs)),
            dma((sets, pairs)),
            dma((sets, half)),
            dma((sets,)),
            dma((sets,)),
            dma((nt, chunks)),
            dma((nt, chunks)),
            dma((nt, chunks)),
        ],
        compiler_params=pltpu.CompilerParams(
            collective_id=0, has_side_effects=True, vmem_limit_bytes=56 * 1024 * 1024
        ),
        cost_estimate=pl.CostEstimate(
            flops=2 * span * weight.shape[0] * (depth + 4 * span),
            bytes_accessed=2 * weight.size + 6 * query.size + 6 * residual.size,
            transcendentals=heads * span * span,
        ),
    )(query, key, value, log_decay, doc_starts, residual, gain.reshape(1, depth), weight)
    return pl.pallas_call(
        write_kernel,
        out_shape=[jax.ShapeDtypeStruct((rows, depth), BF16)] * 2,
        in_specs=[vmem, vmem],
        out_specs=[hbm, hbm],
        scratch_shapes=[dma((2,))],
        cost_estimate=pl.CostEstimate(
            flops=0, bytes_accessed=8 * rows * depth, transcendentals=0
        ),
    )(*outs)


def solution(mesh):
    return jax.shard_map(
        functools.partial(shards, mesh.shape["seq"], mesh.shape["tp"]),
        mesh=mesh,
        in_specs=(
            P("seq", "tp"),
            P("seq", "tp"),
            P("seq", "tp"),
            P("tp", "seq"),
            P("seq", None),
            P(("seq", "tp"), None),
            P("tp", None),
            P(),
        ),
        out_specs=(P(("seq", "tp"), None), P(("seq", "tp"), None)),
        check_vma=False,
    )
```

profile of v0, /device:TPU:23, one launch (start us, length us, event | category | flops | bytes accessed | tf_op | source)
XLA Modules:
  0.0 56.9 jit_solution(12739003889359307239)
XLA Ops:
  0.6 52.5 %shard_map.95 = (bf16[64,4096]{1,0:T(8,128)(2,1)S(1)}, bf16[64,4096]{1,0:T(8,128)(2,1)S(1)}) custom-call(bf16[256,1536]{1,0:T(8,128)(2,1)} %q_hbm.1, bf16[256,1536]{1,0:T(8,128)(2,1)} %k_hbm.1, bf16[256,1536]{1,0:T(8,128)(2,1)} %v_hbm.1, f32[12,256]{1,0:T(8,128)} %decay_hbm.1, s32[1,3]{1,0:T(1,128)} %starts_hbm.1, bf16[64,4096]{1,0:T(8,128)(2,1)} %res_hbm.1, ...), custom_call_target="tpu_custom_call" | custom-call | flops 4026531840 | bytes 16515072 | tf_op jit(solution)/shard_map/pallas_call | solution.py:473
  53.1 0.0 copy-start
  53.1 0.8 %copy-done = bf16[64,4096]{1,0:T(8,128)(2,1)} copy-done((bf16[64,4096]{1,0:T(8,128)(2,1)}, bf16[64,4096]{1,0:T(8,128)(2,1)S(1)}, u32[]{:S(2)}) %copy-start) | copy-done | bytes 524312
  53.9 0.0 copy-start.1
  53.9 0.8 %copy-done.1 = bf16[64,4096]{1,0:T(8,128)(2,1)} copy-done((bf16[64,4096]{1,0:T(8,128)(2,1)}, bf16[64,4096]{1,0:T(8,128)(2,1)S(1)}, u32[]{:S(2)}) %copy-start.1) | copy-done | bytes 524312
  54.7 2.2 %shard_map.96 = (bf16[64,4096]{1,0:T(8,128)(2,1)}, bf16[64,4096]{1,0:T(8,128)(2,1)}) custom-call(bf16[64,4096]{1,0:T(8,128)(2,1)} %copy-done, bf16[64,4096]{1,0:T(8,128)(2,1)} %copy-done.1), custom_call_target="tpu_custom_call" | custom-call | bytes 2097152 | tf_op jit(solution)/shard_map/pallas_call | solution.py:528
Async XLA Ops:
  53.1 0.8 %copy-start = (bf16[64,4096]{1,0:T(8,128)(2,1)}, bf16[64,4096]{1,0:T(8,128)(2,1)S(1)}, u32[]{:S(2)}) copy-start(bf16[64,4096]{1,0:T(8,128)(2,1)S(1)} %get-tuple-element.4.hid_ref) | copy-start | bytes 1572868
  53.9 0.8 %copy-start.1 = (bf16[64,4096]{1,0:T(8,128)(2,1)}, bf16[64,4096]{1,0:T(8,128)(2,1)S(1)}, u32[]{:S(2)}) copy-start(bf16[64,4096]{1,0:T(8,128)(2,1)S(1)} %get-tuple-element.5.norm_ref) | copy-start | bytes 1572868
where the time goes:
time: 57.1 us; the launch traced here: 56.9 us
  Pallas kernels  54.7 us (96%)
  local copies, waits for them, and re-layouts  1.58 us (3%)
  between operations  0.65 us (1%)
    pallas_call x1, Pallas kernels, shards(): pl.pallas_call(functools.partial(kernel, cfg), out_shape=[pltpu.VMEM((row...  52.5 us
    pallas_call x1, Pallas kernels, shards(): pl.pallas_call(write_kernel, out_shape=[jax.ShapeDtypeStruct((rows, depth...  2.18 us
    unnamed x4, local copies, waits for them, and re-layouts  1.58 us

commit v1 on v0

--- a/solution.py
+++ b/solution.py
@@ -10,7 +10,7 @@
 MESH = pl.DeviceIdType.MESH
 F32 = jnp.float32
 BF16 = jnp.bfloat16
-SKEW = 2
+SKEW = 4
 
 
 def _nt(a, b):
@@ -443,17 +443,6 @@
     lax.fori_loop(0, nt * chunks, drain, 0)
 
 
-def write_kernel(hid_ref, norm_ref, hid_hbm, norm_hbm, sem):
-    copies = [
-        pltpu.make_async_copy(hid_ref, hid_hbm, sem.at[0]),
-        pltpu.make_async_copy(norm_ref, norm_hbm, sem.at[1]),
-    ]
-    for copy in copies:
-        copy.start()
-    for copy in copies:
-        copy.wait()
-
-
 def shards(ns, nt, query, key, value, log_decay, doc_starts, residual, weight, gain):
     span = query.shape[0]
     heads = log_decay.shape[0]
@@ -464,13 +453,13 @@
     per = hd // m
     sets = 2 if heads % 2 == 0 else 1
     body = heads // sets * per
-    chunks = 8
+    chunks = 16
     width = depth // chunks
     cfg = (ns, nt, heads, hd, span, m, chunks, width, rows)
     vmem = pl.BlockSpec(memory_space=pltpu.VMEM)
     hbm = pl.BlockSpec(memory_space=pl.ANY)
     dma = pltpu.SemaphoreType.DMA
-    outs = pl.pallas_call(
+    return pl.pallas_call(
         functools.partial(kernel, cfg),
         out_shape=[pltpu.VMEM((rows, depth), BF16)] * 2,
         in_specs=[hbm] * 8,
@@ -525,16 +514,6 @@
             transcendentals=heads * span * span,
         ),
     )(query, key, value, log_decay, doc_starts, residual, gain.reshape(1, depth), weight)
-    return pl.pallas_call(
-        write_kernel,
-        out_shape=[jax.ShapeDtypeStruct((rows, depth), BF16)] * 2,
-        in_specs=[vmem, vmem],
-        out_specs=[hbm, hbm],
-        scratch_shapes=[dma((2,))],
-        cost_estimate=pl.CostEstimate(
-            flops=0, bytes_accessed=8 * rows * depth, transcendentals=0
-        ),
-    )(*outs)
 
 
 def solution(mesh):

time: 57.1 us -> 56.1 us (0.982)
  Pallas kernels: 54.7 us -> 53.7 us
    pallas_call x1 -> x0, Pallas kernels: 2.18 us -> none  [shards(): pl.pallas_call(write_kernel, out_shape=[jax.ShapeDtypeStruct((rows, depth...]
    pallas_call x1, Pallas kernels: 52.5 us -> 53.7 us  [shards(): pl.pallas_call(functools.partial(kernel, cfg), out_shape=[pltpu.VMEM((row...]
    unnamed x4 -> x2, local copies, waits for them, and re-layouts: 1.58 us -> 1.59 us
where the time goes in v1:
time: 56.1 us; the launch traced here: 55.9 us
  Pallas kernels  53.7 us (96%)
  local copies, waits for them, and re-layouts  1.59 us (3%)
  between operations  0.64 us (1%)
    pallas_call x1, Pallas kernels, shards(): pl.pallas_call(functools.partial(kernel, cfg), out_shape=[pltpu.VMEM((row...  53.7 us
    unnamed x2, local copies, waits for them, and re-layouts  1.59 us

profile of v1, /device:TPU:23, one launch (start us, length us, event | category | flops | bytes accessed | tf_op | source)
XLA Modules:
  0.0 55.9 jit_solution(7235215395037567517)
XLA Ops:
  0.6 53.7 %shard_map.95 = (bf16[64,4096]{1,0:T(8,128)(2,1)S(1)}, bf16[64,4096]{1,0:T(8,128)(2,1)S(1)}) custom-call(bf16[256,1536]{1,0:T(8,128)(2,1)} %q_hbm.1, bf16[256,1536]{1,0:T(8,128)(2,1)} %k_hbm.1, bf16[256,1536]{1,0:T(8,128)(2,1)} %v_hbm.1, f32[12,256]{1,0:T(8,128)} %decay_hbm.1, s32[1,3]{1,0:T(1,128)} %starts_hbm.1, bf16[64,4096]{1,0:T(8,128)(2,1)} %res_hbm.1, ...), custom_call_target="tpu_custom_call" | custom-call | flops 4026531840 | bytes 16515072 | tf_op jit(solution)/shard_map/pallas_call | solution.py:462
  54.3 0.8 %copy.12 = bf16[64,4096]{1,0:T(8,128)(2,1)} copy(bf16[64,4096]{1,0:T(8,128)(2,1)S(1)} %get-tuple-element.2) | data formatting | bytes 1048576
  55.1 0.8 %copy.13 = bf16[64,4096]{1,0:T(8,128)(2,1)} copy(bf16[64,4096]{1,0:T(8,128)(2,1)S(1)} %get-tuple-element.3) | data formatting | bytes 1048576

commit v2 on v1

--- a/solution.py
+++ b/solution.py
@@ -10,7 +10,7 @@
 MESH = pl.DeviceIdType.MESH
 F32 = jnp.float32
 BF16 = jnp.bfloat16
-SKEW = 4
+SKEW = 2
 
 
 def _nt(a, b):
@@ -227,11 +227,16 @@
         for o in range(group):
             h = i * group + o
             lanes = pl.ds(pl.multiple_of(h * hd, hd), hd)
-            scores = _nt(q_ref[:, lanes], k_ref[:, lanes])
-            cols = jnp.concatenate([cum_cols[h]] * (span // 128), axis=1)
-            decay = jnp.exp(cols - cum_rows[pl.ds(h, 1), :] + bias[...])
-            weights = (scores * decay).astype(BF16)
-            intra[h] = jnp.dot(weights, v_ref[:, lanes], preferred_element_type=F32)
+            cum_row = cum_rows[pl.ds(h, 1), :]
+            for top in range(0, span, 128):
+                mine, seen = slice(top, top + 128), slice(0, top + 128)
+                scores = _nt(q_ref[mine, lanes], k_ref[seen, lanes])
+                cols = jnp.concatenate([cum_cols[h, mine, :]] * (top // 128 + 1), axis=1)
+                decay = jnp.exp(cols - cum_row[:, seen] + bias[mine, seen])
+                weights = (scores * decay).astype(BF16)
+                intra[h, mine, :] = jnp.dot(
+                    weights, v_ref[seen, lanes], preferred_element_type=F32
+                )
         return 0
 
     def scan(g):
@@ -453,7 +458,7 @@
     per = hd // m
     sets = 2 if heads % 2 == 0 else 1
     body = heads // sets * per
-    chunks = 16
+    chunks = 8
     width = depth // chunks
     cfg = (ns, nt, heads, hd, span, m, chunks, width, rows)
     vmem = pl.BlockSpec(memory_space=pltpu.VMEM)

time: 56.1 us -> 55 us (0.980)
  Pallas kernels: 53.7 us -> 52.5 us
    pallas_call x1, Pallas kernels: 53.7 us -> 52.5 us  [shards(): pl.pallas_call(functools.partial(kernel, cfg), out_shape=[pltpu.VMEM((row...]
where the time goes in v2:
time: 55 us; the launch traced here: 54.7 us
  Pallas kernels  52.5 us (95%)
  local copies, waits for them, and re-layouts  1.59 us (3%)
  between operations  0.64 us (1%)
    pallas_call x1, Pallas kernels, shards(): pl.pallas_call(functools.partial(kernel, cfg), out_shape=[pltpu.VMEM((row...  52.5 us
    unnamed x2, local copies, waits for them, and re-layouts  1.59 us

profile of v2, /device:TPU:23, one launch (start us, length us, event | category | flops | bytes accessed | tf_op | source)
XLA Modules:
  0.0 54.7 jit_solution(17105295110476651872)
XLA Ops:
  0.6 52.5 %shard_map.95 = (bf16[64,4096]{1,0:T(8,128)(2,1)S(1)}, bf16[64,4096]{1,0:T(8,128)(2,1)S(1)}) custom-call(bf16[256,1536]{1,0:T(8,128)(2,1)} %q_hbm.1, bf16[256,1536]{1,0:T(8,128)(2,1)} %k_hbm.1, bf16[256,1536]{1,0:T(8,128)(2,1)} %v_hbm.1, f32[12,256]{1,0:T(8,128)} %decay_hbm.1, s32[1,3]{1,0:T(1,128)} %starts_hbm.1, bf16[64,4096]{1,0:T(8,128)(2,1)} %res_hbm.1, ...), custom_call_target="tpu_custom_call" | custom-call | flops 4026531840 | bytes 16515072 | tf_op jit(solution)/shard_map/pallas_call | solution.py:467
  53.1 0.8 %copy.12 = bf16[64,4096]{1,0:T(8,128)(2,1)} copy(bf16[64,4096]{1,0:T(8,128)(2,1)S(1)} %get-tuple-element.2) | data formatting | bytes 1048576
  53.9 0.8 %copy.13 = bf16[64,4096]{1,0:T(8,128)(2,1)} copy(bf16[64,4096]{1,0:T(8,128)(2,1)S(1)} %get-tuple-element.3) | data formatting | bytes 1048576
